TPU v7x, 256 devices: a whole 4x4x8 slice. The times are simulated.
256 devices in a mesh: slab: 16 (over x, y_hi, core), chan: 16 (over y_lo, z).
Axes of the slice: x: 4, y: 4 (y_hi: 2, y_lo: 2; y = y_hi * 2 + y_lo), z: 8, core: 2. Of those that a mesh axis runs over, the one named last changes fastest.
Arguments:
- density: bfloat16 [256, 32, 16, 128], P('chan', 'slab'), may hold values from -6 to 6
- kernel_one: bfloat16 [256, 3, 3, 3, 256], P('chan'), may hold values from -0.078125 to 0.078125
- bias_one: float32 [256], P('chan'), may hold values from -3 to 3
- kernel_two: bfloat16 [256, 3, 3, 3, 256], P('chan'), may hold values from -0.078125 to 0.078125
- bias_two: float32 [256], P('chan'), may hold values from -3 to 3
Outputs:
- features: float32 [256, 32, 16, 128], P('chan', 'slab')
All inputs are finite; a program needn't handle non-finite values.
Results may differ from a plain program's by a relative error of at most 0.0026.
Values may be sent and summed in bfloat16 or wider, within the bound.
No kernel may reach another device: no remote copies, remote signals or barrier semaphores. Data moves between devices by JAX's collectives and lax.ppermute only.
A program may use at most 128 MiB of HBM per device.

v0:
```python
import functools

import jax
import jax.numpy as jnp
from jax import lax
from jax.experimental import pallas as pl
from jax.experimental.pallas import tpu as pltpu
from jax.sharding import PartitionSpec as P

BF = jnp.bfloat16
F32 = jnp.float32
STRIDE = [[8 * y + z + 2 * p for p in range(4)] for y in range(2) for z in range(2)]
MATE = (0, 1, 8, 9)
CHIP = [(i, i ^ 1) for i in range(16)]
SWAP = [(i, (i + 1) % 16 if i % 2 else (i - 1) % 16) for i in range(16)]
PLANE = (16, 16, 128)
VMEM = 20 * 1024 * 1024


def call(kernel, out_shape, scratch=(), name=None, limit=VMEM, **specs):
    return pl.pallas_call(
        kernel,
        out_shape=out_shape,
        **specs,
        scratch_shapes=list(scratch),
        compiler_params=pltpu.CompilerParams(vmem_limit_bytes=limit),
        name=name,
    )


def first_kernel(density_hbm, one_hbm, two_hbm, bias_one_hbm, bias_two_hbm, *refs):
    outer_ref, inner_ref, *out, density, one, two, bias_one, bias_two, sems = refs
    pairs = (
        (density_hbm, density),
        (one_hbm, one),
        (two_hbm, two),
        (bias_one_hbm, bias_one),
        (bias_two_hbm, bias_two),
    )
    copies = [pltpu.make_async_copy(x, y, sems.at[i]) for i, (x, y) in enumerate(pairs)]
    for copy in copies:
        copy.start()
    core = lax.axis_index("slab") % 2
    me = lax.axis_index("chan")
    place = 2 * (me // 8) + me % 2
    row = lax.broadcasted_iota(jnp.int32, (256, 256), 0)
    col = lax.broadcasted_iota(jnp.int32, (256, 256), 1)
    y, p, z, c = row // 128, (row // 32) % 4, (row // 16) % 2, row % 16
    move = jnp.where(col == ((2 * y + z) ^ place) * 64 + p * 16 + c, 1.0, 0.0).astype(BF)
    copies[0].wait()
    outer_ref[...] = jnp.swapaxes(density[:, core], 0, 1)
    inner_ref[...] = jnp.swapaxes(density[:, 1 - core], 0, 1)
    for k, ref in enumerate((one, two)):
        copies[1 + k].wait()
        for a in range(3):
            taps = ref[a + core * (2 - 2 * a)].reshape(144, 256)
            moved = jnp.dot(taps, move, preferred_element_type=F32).astype(BF)
            for b in range(3):
                for e in range(3):
                    tap = (3 * b + e) * 16
                    at = (3 * a + e) * 64
                    for d in range(4):
                        out[d][k, b, :, at : at + 64] = moved[tap : tap + 16, d * 64 : d * 64 + 64]
    row = lax.broadcasted_iota(jnp.int32, (16, 16), 0)
    col = lax.broadcasted_iota(jnp.int32, (16, 16), 1)
    for k, ref in enumerate((bias_one, bias_two)):
        copies[3 + k].wait()
        bias = jnp.sum(jnp.where(row == col, ref[...], 0.0), axis=1, keepdims=True)
        out[4 + k][...] = jnp.broadcast_to(bias, (16, 128))


def lay(ref, cols, a):
    for y in range(16):
        tile = ref[:, y].reshape(64, 128)
        at = slice(y * 128, y * 128 + 128)
        cols[a * 192 : a * 192 + 64, at] = pltpu.roll(tile, 1, 1)
        cols[a * 192 + 64 : a * 192 + 128, at] = tile
        cols[a * 192 + 128 : a * 192 + 192, at] = pltpu.roll(tile, 127, 1)


def matrix(which, w_refs):
    return jnp.concatenate([w[which].reshape(48, 576) for w in w_refs], axis=0)


def fold(rows, outs, plane):
    for d, out in enumerate(outs):
        for y in range(16):
            total = None
            for b in range(3):
                at = ((y + b - 1) % 16) * 128
                part = rows[d * 48 + b * 16 : d * 48 + b * 16 + 16, at : at + 128]
                total = part if total is None else total + part
            out[plane, y] = total.astype(out.dtype)


def outside_kernel(which, main_ref, w0, w1, w2, w3, r0, r1, r2, r3, part, cols, rows):
    for a, p in enumerate((2, 0, 1)):
        lay(main_ref.at[:, p], cols, a)
    w = matrix(which, (w0, w1, w2, w3))
    rows[...] = jnp.dot(w, cols[...], preferred_element_type=F32)
    fold(rows, (r0, r1, r2, r3), 0)
    part[...] = jnp.dot(w[:, :384], cols[192:576, :], preferred_element_type=F32)


def first_outside_kernel(main_ref, w0, w1, w2, w3, r0, r1, r2, r3, cols, rows):
    for a, p in enumerate((2, 0, 1)):
        lay(main_ref.at[:, p], cols, a)
    w = matrix(0, (w0, w1, w2, w3))
    rows[...] = jnp.dot(w, cols[...], preferred_element_type=F32)
    fold(rows, (r0, r1, r2, r3), 0)


def inside_kernel(which, plane, share, beside_ref, w0, w1, w2, w3, *refs):
    r0, r1, r2, r3, side, rows = refs[4 * plane :]
    lay(beside_ref, side, 0)
    w = matrix(which, (w0, w1, w2, w3))
    if which:
        most = share[...]
    else:
        most = jnp.dot(w[:, :384], share[192:576, :], preferred_element_type=F32)
    rows[...] = most + jnp.dot(w[:, 384:], side[...], preferred_element_type=F32)
    fold(rows, (r0, r1, r2, r3), plane)


def join_kernel(outer_ref, inner_ref, beyond_ref, out_ref):
    out_ref[0] = outer_ref[...]
    out_ref[1] = inner_ref[...]
    out_ref[2] = beyond_ref[...]


def leaky(parts, bias_ref):
    total = bias_ref[...]
    for part in parts:
        total = total + part[0].astype(F32)
    return jnp.where(total >= 0.0, total, 0.3 * total).astype(BF)


def outer_kernel(p0, p1, p2, p3, bias_ref, out_ref):
    out_ref[...] = leaky((p0, p1, p2, p3), bias_ref)


def inner_kernel(p0, p1, p2, p3, bias_ref, outer_ref, beyond_ref, out_ref):
    out_ref[0] = outer_ref[...]
    out_ref[1] = leaky((p0, p1, p2, p3), bias_ref)
    out_ref[2] = beyond_ref[...]


def features_kernel(p0, p1, p2, p3, bias_ref, out_ref):
    core = lax.axis_index("slab") % 2
    for o in range(2):
        total = p0[o] + bias_ref[...]
        for part in (p1, p2, p3):
            total = total + part[o].astype(F32)
        out_ref[:, core + o * (1 - 2 * core)] = jnp.swapaxes(total, 0, 1)


def exchange(blocks):
    return [blocks[0]] + [
        lax.ppermute(blocks[d], "chan", [(i, i ^ MATE[d]) for i in range(16)]) for d in (1, 2, 3)
    ]


def gather(planes):
    return lax.all_gather(planes, "chan", axis=0, axis_index_groups=STRIDE)


def swap(outer):
    return lax.ppermute(outer, "slab", SWAP)


def sums(planes, dtype):
    return [jax.ShapeDtypeStruct((planes,) + PLANE, t) for t in (F32, dtype, dtype, dtype)]


def outside(which, planes, dtype, *operands):
    cols, rows = pltpu.VMEM((576, 2048), BF), pltpu.VMEM((192, 2048), F32)
    *parts, share = call(
        functools.partial(outside_kernel, which) if which else first_outside_kernel,
        sums(planes, dtype)
        + [jax.ShapeDtypeStruct((192, 2048), F32) if which else jax.ShapeDtypeStruct((576, 2048), BF)],
        [cols, rows] if which else [rows],
        name="outside",
    )(*operands)
    return parts, share


def inside(which, planes, dtype, *operands, **more):
    return call(
        functools.partial(inside_kernel, which, planes - 1),
        sums(planes, dtype),
        [pltpu.VMEM((192, 2048), BF), pltpu.VMEM((192, 2048), F32)],
        name="inside",
        **more,
    )(*operands)


def body(density, kernel_one, bias_one, kernel_two, bias_two):
    plane = jax.ShapeDtypeStruct(PLANE, BF)
    taps = pltpu.VMEM((3, 3, 3, 16, 256), BF)
    row = pltpu.VMEM((1, 16), F32)
    outer, inner, *w, bias_one, bias_two = call(
        first_kernel,
        [pltpu.VMEM(PLANE, BF)] * 2
        + [pltpu.VMEM((2, 3, 16, 576), BF)] * 4
        + [pltpu.VMEM((16, 128), F32)] * 2,
        [pltpu.VMEM((16, 2, 16, 128), BF), taps, taps, row, row, pltpu.SemaphoreType.DMA((5,))],
        name="first",
        in_specs=[pl.BlockSpec(memory_space=pltpu.HBM)] * 5,
    )(
        *(
            pltpu.with_memory_space_constraint(x, pltpu.HBM)
            for x in (
                density,
                jnp.transpose(kernel_one, (1, 2, 3, 0, 4)),
                jnp.transpose(kernel_two, (1, 2, 3, 0, 4)),
                bias_one[None],
                bias_two[None],
            )
        )
    )
    beyond = swap(outer)
    w = exchange(w)
    joined = jax.ShapeDtypeStruct((3,) + PLANE, BF)
    main = gather(call(join_kernel, joined, name="join")(outer, inner, beyond))
    w[1:], main = lax.optimization_barrier((w[1:], main))
    beside = lax.ppermute(main[:, 1], "slab", CHIP)
    parts_outer, cols = outside(0, 1, BF, main, *w)
    parts_outer = exchange(parts_outer)
    parts_inner = exchange(inside(0, 1, F32, cols, beside, *w))
    outer = call(outer_kernel, plane, name="outer")(*parts_outer, bias_one)
    beyond = swap(outer)
    main = gather(call(inner_kernel, joined, name="inner")(*parts_inner, bias_one, outer, beyond))
    beside = lax.ppermute(main[:, 1], "slab", CHIP)
    parts, cols = outside(1, 2, BF, main, *w)
    same = {6 + d: d for d in range(4)}
    parts = exchange(inside(1, 2, BF, cols, beside, *w, *parts, input_output_aliases=same))
    return call(features_kernel, jax.ShapeDtypeStruct((16, 2, 16, 128), F32), name="features")(
        *parts, bias_two
    )


def solution(mesh):
    return jax.shard_map(
        body,
        mesh=mesh,
        in_specs=(
            P("chan", "slab", None, None),
            P("chan", None, None, None, None),
            P("chan"),
            P("chan", None, None, None, None),
            P("chan"),
        ),
        out_specs=P("chan", "slab", None, None),
        check_vma=False,
    )
```

profile of v0, /device:TPU:2, one launch (start us, length us, event | category | flops | bytes accessed | tf_op | source)
XLA Modules:
  0.0 80.3 jit_solution(9631735176160434984)
XLA Ops:
  0.0 1.9 %first.1 = (bf16[16,16,128]{2,1,0:T(8,128)(2,1)S(1)}, bf16[16,16,128]{2,1,0:T(8,128)(2,1)S(1)}, bf16[2,3,16,576]{3,2,1,0:T(8,128)(2,1)S(1)}, bf16[2,3,16,576]{3,...) custom-call(bf16[16,2,16,128]{3,2,1,0:T(8,128)(2,1)} %density_hbm.1,, ...), custom_call_target="tpu_custom_call" | custom-call | tf_op jit(solution)/shard_map/first/pallas_call | solution.py:201
  1.9 2.7 %collective-permute-start.3 = (bf16[16,16,128]{2,1,0:T(8,128)(2,1)S(1)}, bf16[16,16,128]{2,1,0:T(8,128)(2,1)S(1)}, u32[]{:S(2)}, u32[]{:S(2)}) collective-permute-start(bf16[16,16,128]{2,1,0:T(8,128)(2,1)S(1)} %get-tuple-element.38.outer_ref), channel_id=1, source_target_pairs={{0,240},{16,32},{32,16},{48,64},{64,48},{80,96},{96,80},{112,128},... | collective-permute-start | bytes 196616 | tf_op jit(solution)/shard_map/ppermute | solution.py:168
  4.6 1.9 %collective-permute-start = (bf16[2,3,16,576]{3,2,1,0:T(8,128)(2,1)S(1)}, bf16[2,3,16,576]{3,2,1,0:T(8,128)(2,1)S(1)}, u32[]{:S(2)}, u32[]{:S(2)}) collective-permute-start(bf16[2,3,16,576]{3,2,1,0:T(8,128)(2,1)S(1)} %get-tuple-element.35), channel_id=1, source_target_pairs={{0,1},{1,0},{2,3},{3,2},{4,5},{5,4},{6,7},{7,6},{8,9},{9,8},{10,11... | collective-permute-start | bytes 331784 | tf_op jit(solution)/shard_map/ppermute | solution.py:159
  6.5 0.7 collective-permute-start.1
  7.2 0.9 %collective-permute-start.2 = (bf16[2,3,16,576]{3,2,1,0:T(8,128)(2,1)S(1)}, bf16[2,3,16,576]{3,2,1,0:T(8,128)(2,1)S(1)}, u32[]{:S(2)}, u32[]{:S(2)}) collective-permute-start(bf16[2,3,16,576]{3,2,1,0:T(8,128)(2,1)S(1)} %get-tuple-element.37), channel_id=1, source_target_pairs={{0,9},{1,8},{2,11},{3,10},{4,13},{5,12},{6,15},{7,14},{8,1},{9,0},... | collective-permute-start | bytes 331784 | tf_op jit(solution)/shard_map/ppermute | solution.py:159
  8.1 0.0 collective-permute-done.3.beyond_ref
  8.1 24.8 %all-gather = bf16[12,16,16,128]{3,2,1,0:T(8,128)(2,1)S(1)} all-gather(bf16[3,16,16,128]{3,2,1,0:T(8,128)(2,1)S(1)} %join.1), channel_id=2, replica_groups={{0,2,4,6},{1,3,5,7},{8,10,12,14},{9,11,13,15},{16,18,20,22},{17,19,21,2..., dimensions={0}, use_global_device_ids=true | all-gather | bytes 983040 | tf_op jit(solution)/shard_map/all_gather | solution.py:164
  32.9 0.0 collective-permute-done.w1
  32.9 0.0 collective-permute-done.1.w2
  32.9 0.0 collective-permute-done.2.w3
  33.0 0.1 collective-permute-start.4
  33.1 0.9 %outside.2 = (f32[1,16,16,128]{3,2,1,0:T(8,128)S(1)}, bf16[1,16,16,128]{3,2,1,0:T(8,128)(2,1)S(1)}, bf16[1,16,16,128]{3,2,1,0:T(8,128)(2,1)S(1)}, bf16[1,16,16,1...) custom-call(bf16[4,3,16,16,128]{4,3,2,1,0:T(8,128)(2,1)S(1)} %bitcast.13, bf16[2,3,16,576]{3,2,1,0:T(8,128)(2,1)S(1)} %get-tuple-element.41.w0, ...), custom_call_target="tpu_custom_call" | custom-call | tf_op jit(solution)/shard_map/outside/pallas_call | solution.py:177
  34.0 0.1 collective-permute-start.10
  34.1 1.5 %collective-permute-start.8 = (bf16[1,16,16,128]{3,2,1,0:T(8,128)(2,1)S(1)}, bf16[1,16,16,128]{3,2,1,0:T(8,128)(2,1)S(1)}, u32[]{:S(2)}, u32[]{:S(2)}) collective-permute-start(bf16[1,16,16,128]{3,2,1,0:T(8,128)(2,1)S(1)} %get-tuple-element.52), channel_id=1, source_target_pairs={{0,1},{1,0},{2,3},{3,2},{4,5},{5,4},{6,7},{7,6},{8,9},{9,8},{10,11... | collective-permute-start | bytes 196616 | tf_op jit(solution)/shard_map/ppermute | solution.py:159
  35.6 2.0 %collective-permute-start.9 = (bf16[1,16,16,128]{3,2,1,0:T(8,128)(2,1)S(1)}, bf16[1,16,16,128]{3,2,1,0:T(8,128)(2,1)S(1)}, u32[]{:S(2)}, u32[]{:S(2)}) collective-permute-start(bf16[1,16,16,128]{3,2,1,0:T(8,128)(2,1)S(1)} %get-tuple-element.53), channel_id=1, source_target_pairs={{0,8},{1,9},{2,10},{3,11},{4,12},{5,13},{6,14},{7,15},{8,0},{9,1},... | collective-permute-start | bytes 196616 | tf_op jit(solution)/shard_map/ppermute | solution.py:159
  37.6 0.0 collective-permute-done.4.beside_ref
  37.6 0.9 %inside.2 = (f32[1,16,16,128]{3,2,1,0:T(8,128)S(1)}, f32[1,16,16,128]{3,2,1,0:T(8,128)S(1)}, f32[1,16,16,128]{3,2,1,0:T(8,128)S(1)}, f32[1,16,16,128]{3,2,1,0:T(8,128)S(1)}) custom-call(bf16[576,2048]{1,0:T(8,128)(2,1)S(1)} %get-tuple-element.45.share, bf16[4,16,16,128]{3,2,1,0:T(8,128)(2,1)S(1)} %collective-permute-done.4.beside_ref, ...), custom_call_target="tpu_custom_call" | custom-call | tf_op jit(solution)/shard_map/inside/pallas_call | solution.py:188
  38.5 0.1 collective-permute-start.5
  38.6 0.7 collective-permute-start.6
  39.2 0.6 collective-permute-done.10.p3
  39.9 2.2 %collective-permute-start.7 = (f32[1,16,16,128]{3,2,1,0:T(8,128)S(1)}, f32[1,16,16,128]{3,2,1,0:T(8,128)S(1)}, u32[]{:S(2)}, u32[]{:S(2)}) collective-permute-start(f32[1,16,16,128]{3,2,1,0:T(8,128)S(1)} %get-tuple-element.49), channel_id=1, source_target_pairs={{0,9},{1,8},{2,11},{3,10},{4,13},{5,12},{6,15},{7,14},{8,1},{9,0},... | collective-permute-start | bytes 393224 | tf_op jit(solution)/shard_map/ppermute | solution.py:159
  42.1 0.0 collective-permute-done.8.p1
  42.1 0.0 collective-permute-done.9.p2
  42.1 0.1 outer.1.outer_ref
  42.1 0.1 collective-permute-start.11
  42.2 6.2 %collective-permute-done.11.beyond_ref = bf16[16,16,128]{2,1,0:T(8,128)(2,1)S(1)} collective-permute-done((bf16[16,16,128]{2,1,0:T(8,128)(2,1)S(1)}, bf16[16,16,128]{2,1,0:T(8,128)(2,1)S(1)}, u32[]{:S(2)}, u32[]{:S(2)}) %collective-permute-start.11) | collective-permute-done | bytes 65568 | tf_op jit(solution)/shard_map/ppermute | solution.py:168
  48.4 0.0 collective-permute-done.5.p1
  48.4 0.0 collective-permute-done.6.p2
  48.4 0.0 collective-permute-done.7.p3
  48.4 0.1 inner.1
  48.5 20.1 %all-gather.1 = bf16[12,16,16,128]{3,2,1,0:T(8,128)(2,1)S(1)} all-gather(bf16[3,16,16,128]{3,2,1,0:T(8,128)(2,1)S(1)} %inner.1), channel_id=3, replica_groups={{0,2,4,6},{1,3,5,7},{8,10,12,14},{9,11,13,15},{16,18,20,22},{17,19,21,2..., dimensions={0}, use_global_device_ids=true | all-gather | bytes 983040 | tf_op jit(solution)/shard_map/all_gather | solution.py:164
  68.6 0.1 collective-permute-start.12
  68.7 1.3 %outside.3 = (f32[2,16,16,128]{3,2,1,0:T(8,128)S(1)}, bf16[2,16,16,128]{3,2,1,0:T(8,128)(2,1)S(1)}, bf16[2,16,16,128]{3,2,1,0:T(8,128)(2,1)S(1)}, bf16[2,16,16,128]{3,2,1,0:T(8,128)(2,1)S(1)}, f32[192,2048]{1,0:T(8,128)S(1)}) custom-call(bf16[4,3,16,16,128]{4,3,2,1,0:T(8,128)(2,1)S(1)} %bitcast.15, bf16[2,3,16,576]{3,2,1,0:T(8,128)(2,1)S(1)} %get-tuple-element.41.w0, ...), custom_call_target="tpu_custom_call" | custom-call | tf_op jit(solution)/shard_map/outside/pallas_call | solution.py:177
  70.1 0.2 collective-permute-done.12.beside_ref
  70.3 0.5 inside.3
  70.7 0.1 collective-permute-start.13
  70.9 0.3 collective-permute-start.14
  71.1 3.2 %collective-permute-start.15 = (bf16[2,16,16,128]{3,2,1,0:T(8,128)(2,1)S(1)}, bf16[2,16,16,128]{3,2,1,0:T(8,128)(2,1)S(1)}, u32[]{:S(2)}, u32[]{:S(2)}) collective-permute-start(bf16[2,16,16,128]{3,2,1,0:T(8,128)(2,1)S(1)} %get-tuple-element.63), channel_id=1, source_target_pairs={{0,9},{1,8},{2,11},{3,10},{4,13},{5,12},{6,15},{7,14},{8,1},{9,0},... | collective-permute-start | bytes 393224 | tf_op jit(solution)/shard_map/ppermute | solution.py:159
  74.3 2.8 %collective-permute-done.13.p1 = bf16[2,16,16,128]{3,2,1,0:T(8,128)(2,1)S(1)} collective-permute-done((bf16[2,16,16,128]{3,2,1,0:T(8,128)(2,1)S(1)}, bf16[2,16,16,128]{3,2,1,0:T(8,128)(2,1)S(1)}, u32[]{:S(2)}, u32[]{:S(2)}) %collective-permute-start.13) | collective-permute-done | bytes 131104 | tf_op jit(solution)/shard_map/ppermute | solution.py:159
  77.2 2.3 %collective-permute-done.14.p2 = bf16[2,16,16,128]{3,2,1,0:T(8,128)(2,1)S(1)} collective-permute-done((bf16[2,16,16,128]{3,2,1,0:T(8,128)(2,1)S(1)}, bf16[2,16,16,128]{3,2,1,0:T(8,128)(2,1)S(1)}, u32[]{:S(2)}, u32[]{:S(2)}) %collective-permute-start.14) | collective-permute-done | bytes 131104 | tf_op jit(solution)/shard_map/ppermute | solution.py:159
  79.5 0.0 collective-permute-done.15.p3
  79.5 0.8 %features.1 = f32[16,2,16,128]{3,2,1,0:T(8,128)} custom-call(f32[2,16,16,128]{3,2,1,0:T(8,128)S(1)} %get-tuple-element.60.p0, bf16[2,16,16,128]{3,2,1,0:T(8,128)(2,1)S(1)} %collective-permute-done.13.p1, bf16[2,16,16,128]{3,2,1,0:T(8,128)(2,1)S(1)} %collective-permute-done.14.p2, bf16[2,16,16,128]{3,2,1,0:T(8,128)(2,1)S(1)} %collective-permute-done.15.p3, ...), custom_call_target="tpu_custom_call" | custom-call | tf_op jit(solution)/shard_map/features/pallas_call | solution.py:237
  (3 shorter events, 0.1 us)
Async XLA Ops:
  1.9 6.2 %collective-permute-start.3 = (bf16[16,16,128]{2,1,0:T(8,128)(2,1)S(1)}, bf16[16,16,128]{2,1,0:T(8,128)(2,1)S(1)}, u32[]{:S(2)}, u32[]{:S(2)}) collective-permute-start(bf16[16,16,128]{2,1,0:T(8,128)(2,1)S(1)} %get-tuple-element.38.outer_ref), channel_id=1, source_target_pairs={{0,240},{16,32},{32,16},{48,64},{64,48},{80,96},{96,80},{112,128},... | collective-permute-start | bytes 196616 | tf_op jit(solution)/shard_map/ppermute | solution.py:168
  4.6 28.4 %collective-permute-start = (bf16[2,3,16,576]{3,2,1,0:T(8,128)(2,1)S(1)}, bf16[2,3,16,576]{3,2,1,0:T(8,128)(2,1)S(1)}, u32[]{:S(2)}, u32[]{:S(2)}) collective-permute-start(bf16[2,3,16,576]{3,2,1,0:T(8,128)(2,1)S(1)} %get-tuple-element.35), channel_id=1, source_target_pairs={{0,1},{1,0},{2,3},{3,2},{4,5},{5,4},{6,7},{7,6},{8,9},{9,8},{10,11... | collective-permute-start | bytes 331784 | tf_op jit(solution)/shard_map/ppermute | solution.py:159
  6.5 26.4 %collective-permute-start.1 = (bf16[2,3,16,576]{3,2,1,0:T(8,128)(2,1)S(1)}, bf16[2,3,16,576]{3,2,1,0:T(8,128)(2,1)S(1)}, u32[]{:S(2)}, u32[]{:S(2)}) collective-permute-start(bf16[2,3,16,576]{3,2,1,0:T(8,128)(2,1)S(1)} %get-tuple-element.36), channel_id=1, source_target_pairs={{0,8},{1,9},{2,10},{3,11},{4,12},{5,13},{6,14},{7,15},{8,0},{9,1},... | collective-permute-start | bytes 331784 | tf_op jit(solution)/shard_map/ppermute | solution.py:159
  7.2 25.8 %collective-permute-start.2 = (bf16[2,3,16,576]{3,2,1,0:T(8,128)(2,1)S(1)}, bf16[2,3,16,576]{3,2,1,0:T(8,128)(2,1)S(1)}, u32[]{:S(2)}, u32[]{:S(2)}) collective-permute-start(bf16[2,3,16,576]{3,2,1,0:T(8,128)(2,1)S(1)} %get-tuple-element.37), channel_id=1, source_target_pairs={{0,9},{1,8},{2,11},{3,10},{4,13},{5,12},{6,15},{7,14},{8,1},{9,0},... | collective-permute-start | bytes 331784 | tf_op jit(solution)/shard_map/ppermute | solution.py:159
  33.0 4.6 %collective-permute-start.4 = (bf16[4,16,16,128]{3,2,1,0:T(8,128)(2,1)S(1)}, bf16[4,16,16,128]{3,2,1,0:T(8,128)(2,1)S(1)}, u32[]{:S(2)}, u32[]{:S(2)}) collective-permute-start(bf16[4,16,16,128]{3,2,1,0:T(8,128)(2,1)S(1)} %slice_bitcast_fusion.1), channel_id=1, source_target_pairs={{0,16},{16,0},{32,48},{48,32},{64,80},{80,64},{96,112},{112,96},{1... | collective-permute-start | bytes 786440 | tf_op jit(solution)/shard_map/ppermute | solution.py:226
  34.0 5.9 %collective-permute-start.10 = (bf16[1,16,16,128]{3,2,1,0:T(8,128)(2,1)S(1)}, bf16[1,16,16,128]{3,2,1,0:T(8,128)(2,1)S(1)}, u32[]{:S(2)}, u32[]{:S(2)}) collective-permute-start(bf16[1,16,16,128]{3,2,1,0:T(8,128)(2,1)S(1)} %get-tuple-element.54), channel_id=1, source_target_pairs={{0,9},{1,8},{2,11},{3,10},{4,13},{5,12},{6,15},{7,14},{8,1},{9,0},... | collective-permute-start | bytes 196616 | tf_op jit(solution)/shard_map/ppermute | solution.py:159
  34.1 8.0 %collective-permute-start.8 = (bf16[1,16,16,128]{3,2,1,0:T(8,128)(2,1)S(1)}, bf16[1,16,16,128]{3,2,1,0:T(8,128)(2,1)S(1)}, u32[]{:S(2)}, u32[]{:S(2)}) collective-permute-start(bf16[1,16,16,128]{3,2,1,0:T(8,128)(2,1)S(1)} %get-tuple-element.52), channel_id=1, source_target_pairs={{0,1},{1,0},{2,3},{3,2},{4,5},{5,4},{6,7},{7,6},{8,9},{9,8},{10,11... | collective-permute-start | bytes 196616 | tf_op jit(solution)/shard_map/ppermute | solution.py:159
  35.6 6.5 %collective-permute-start.9 = (bf16[1,16,16,128]{3,2,1,0:T(8,128)(2,1)S(1)}, bf16[1,16,16,128]{3,2,1,0:T(8,128)(2,1)S(1)}, u32[]{:S(2)}, u32[]{:S(2)}) collective-permute-start(bf16[1,16,16,128]{3,2,1,0:T(8,128)(2,1)S(1)} %get-tuple-element.53), channel_id=1, source_target_pairs={{0,8},{1,9},{2,10},{3,11},{4,12},{5,13},{6,14},{7,15},{8,0},{9,1},... | collective-permute-start | bytes 196616 | tf_op jit(solution)/shard_map/ppermute | solution.py:159
  38.5 9.9 %collective-permute-start.5 = (f32[1,16,16,128]{3,2,1,0:T(8,128)S(1)}, f32[1,16,16,128]{3,2,1,0:T(8,128)S(1)}, u32[]{:S(2)}, u32[]{:S(2)}) collective-permute-start(f32[1,16,16,128]{3,2,1,0:T(8,128)S(1)} %get-tuple-element.47), channel_id=1, source_target_pairs={{0,1},{1,0},{2,3},{3,2},{4,5},{5,4},{6,7},{7,6},{8,9},{9,8},{10,11... | collective-permute-start | bytes 393224 | tf_op jit(solution)/shard_map/ppermute | solution.py:159
  38.6 9.8 %collective-permute-start.6 = (f32[1,16,16,128]{3,2,1,0:T(8,128)S(1)}, f32[1,16,16,128]{3,2,1,0:T(8,128)S(1)}, u32[]{:S(2)}, u32[]{:S(2)}) collective-permute-start(f32[1,16,16,128]{3,2,1,0:T(8,128)S(1)} %get-tuple-element.48), channel_id=1, source_target_pairs={{0,8},{1,9},{2,10},{3,11},{4,12},{5,13},{6,14},{7,15},{8,0},{9,1},... | collective-permute-start | bytes 393224 | tf_op jit(solution)/shard_map/ppermute | solution.py:159
  39.9 8.5 %collective-permute-start.7 = (f32[1,16,16,128]{3,2,1,0:T(8,128)S(1)}, f32[1,16,16,128]{3,2,1,0:T(8,128)S(1)}, u32[]{:S(2)}, u32[]{:S(2)}) collective-permute-start(f32[1,16,16,128]{3,2,1,0:T(8,128)S(1)} %get-tuple-element.49), channel_id=1, source_target_pairs={{0,9},{1,8},{2,11},{3,10},{4,13},{5,12},{6,15},{7,14},{8,1},{9,0},... | collective-permute-start | bytes 393224 | tf_op jit(solution)/shard_map/ppermute | solution.py:159
  42.1 6.3 %collective-permute-start.11 = (bf16[16,16,128]{2,1,0:T(8,128)(2,1)S(1)}, bf16[16,16,128]{2,1,0:T(8,128)(2,1)S(1)}, u32[]{:S(2)}, u32[]{:S(2)}) collective-permute-start(bf16[16,16,128]{2,1,0:T(8,128)(2,1)S(1)} %outer.1.outer_ref), channel_id=1, source_target_pairs={{0,240},{16,32},{32,16},{48,64},{64,48},{80,96},{96,80},{112,128},... | collective-permute-start | bytes 196616 | tf_op jit(solution)/shard_map/ppermute | solution.py:168
  68.6 1.6 %collective-permute-start.12 = (bf16[4,16,16,128]{3,2,1,0:T(8,128)(2,1)S(1)}, bf16[4,16,16,128]{3,2,1,0:T(8,128)(2,1)S(1)}, u32[]{:S(2)}, u32[]{:S(2)}) collective-permute-start(bf16[4,16,16,128]{3,2,1,0:T(8,128)(2,1)S(1)} %slice_bitcast_fusion), channel_id=1, source_target_pairs={{0,16},{16,0},{32,48},{48,32},{64,80},{80,64},{96,112},{112,96},{1... | collective-permute-start | bytes 786440 | tf_op jit(solution)/shard_map/ppermute | solution.py:233
  70.7 6.4 %collective-permute-start.13 = (bf16[2,16,16,128]{3,2,1,0:T(8,128)(2,1)S(1)}, bf16[2,16,16,128]{3,2,1,0:T(8,128)(2,1)S(1)}, u32[]{:S(2)}, u32[]{:S(2)}) collective-permute-start(bf16[2,16,16,128]{3,2,1,0:T(8,128)(2,1)S(1)} %get-tuple-element.61), channel_id=1, source_target_pairs={{0,1},{1,0},{2,3},{3,2},{4,5},{5,4},{6,7},{7,6},{8,9},{9,8},{10,11... | collective-permute-start | bytes 393224 | tf_op jit(solution)/shard_map/ppermute | solution.py:159
  70.9 8.6 %collective-permute-start.14 = (bf16[2,16,16,128]{3,2,1,0:T(8,128)(2,1)S(1)}, bf16[2,16,16,128]{3,2,1,0:T(8,128)(2,1)S(1)}, u32[]{:S(2)}, u32[]{:S(2)}) collective-permute-start(bf16[2,16,16,128]{3,2,1,0:T(8,128)(2,1)S(1)} %get-tuple-element.62), channel_id=1, source_target_pairs={{0,8},{1,9},{2,10},{3,11},{4,12},{5,13},{6,14},{7,15},{8,0},{9,1},... | collective-permute-start | bytes 393224 | tf_op jit(solution)/shard_map/ppermute | solution.py:159
  71.1 8.4 %collective-permute-start.15 = (bf16[2,16,16,128]{3,2,1,0:T(8,128)(2,1)S(1)}, bf16[2,16,16,128]{3,2,1,0:T(8,128)(2,1)S(1)}, u32[]{:S(2)}, u32[]{:S(2)}) collective-permute-start(bf16[2,16,16,128]{3,2,1,0:T(8,128)(2,1)S(1)} %get-tuple-element.63), channel_id=1, source_target_pairs={{0,9},{1,8},{2,11},{3,10},{4,13},{5,12},{6,15},{7,14},{8,1},{9,0},... | collective-permute-start | bytes 393224 | tf_op jit(solution)/shard_map/ppermute | solution.py:159
where the time goes:
time: 81.8 us; the launch traced here: 80.3 us
  blocking collectives  44.9 us (55%)
  starting transfers between devices  16.5 us (20%)
  waiting for transfers between devices  12.2 us (15%)
  Pallas kernels  6.45 us (8%)
    all_gather x2, blocking collectives, gather(): return lax.all_gather(planes, 'chan', axis=0, axis_index_groups=STRIDE)  44.9 us
    ppermute x12, starting transfers between devices, exchange(): lax.ppermute(blocks[d], 'chan', [(i, i ^ MATE[d]) for i in range(16)])  13.6 us
    ppermute x2, waiting for transfers between devices, swap(): return lax.ppermute(outer, 'slab', SWAP)  6.24 us
    ppermute x12, waiting for transfers between devices, exchange(): lax.ppermute(blocks[d], 'chan', [(i, i ^ MATE[d]) for i in range(16)])  5.83 us
    ppermute x2, starting transfers between devices, swap(): return lax.ppermute(outer, 'slab', SWAP)  2.78 us
    pallas_call x2, Pallas kernels, outside(): call(functools.partial(outside_kernel, which) if which else first_outside...  2.26 us
    pallas_call x1, Pallas kernels, body(): call(first_kernel, [pltpu.VMEM(PLANE, BF)] * 2 + [pltpu.VMEM((2, 3, 16, 5...  1.88 us
  transfers between devices with their start and end apart: 16, of which 5 were waited for; matrix products, arithmetic and copies ran while one was open for 0% of the time, Pallas kernels for 4%

commit v1 on v0

--- a/solution.py
+++ b/solution.py
@@ -154,10 +154,11 @@
         out_ref[:, core + o * (1 - 2 * core)] = jnp.swapaxes(total, 0, 1)
 
 
-def exchange(blocks):
-    return [blocks[0]] + [
-        lax.ppermute(blocks[d], "chan", [(i, i ^ MATE[d]) for i in range(16)]) for d in (1, 2, 3)
-    ]
+def exchange(blocks, order=(1, 2, 3)):
+    got = {
+        d: lax.ppermute(blocks[d], "chan", [(i, i ^ MATE[d]) for i in range(16)]) for d in order
+    }
+    return [blocks[0]] + [got[d] for d in (1, 2, 3)]
 
 
 def gather(planes):
@@ -219,7 +220,7 @@
         )
     )
     beyond = swap(outer)
-    w = exchange(w)
+    w = exchange(w, (3, 2, 1))
     joined = jax.ShapeDtypeStruct((3,) + PLANE, BF)
     main = gather(call(join_kernel, joined, name="join")(outer, inner, beyond))
     w[1:], main = lax.optimization_barrier((w[1:], main))

time: 81.8 us -> 81.8 us (level)
  no operation moved by 1% of the time
where the time goes in v1:
time: 81.8 us; the launch traced here: 80.3 us
  blocking collectives  44.9 us (55%)
  starting transfers between devices  16.5 us (20%)
  waiting for transfers between devices  12.2 us (15%)
  Pallas kernels  6.45 us (8%)
    all_gather x2, blocking collectives, gather(): return lax.all_gather(planes, 'chan', axis=0, axis_index_groups=STRIDE)  44.9 us
    ppermute x12, starting transfers between devices, exchange(): lax.ppermute(blocks[d], 'chan', [(i, i ^ MATE[d]) for i in range(16)])  13.6 us
    ppermute x2, waiting for transfers between devices, swap(): return lax.ppermute(outer, 'slab', SWAP)  6.24 us
    ppermute x12, waiting for transfers between devices, exchange(): lax.ppermute(blocks[d], 'chan', [(i, i ^ MATE[d]) for i in range(16)])  5.83 us
    ppermute x2, starting transfers between devices, swap(): return lax.ppermute(outer, 'slab', SWAP)  2.78 us
    pallas_call x2, Pallas kernels, outside(): call(functools.partial(outside_kernel, which) if which else first_outside...  2.26 us
    pallas_call x1, Pallas kernels, body(): call(first_kernel, [pltpu.VMEM(PLANE, BF)] * 2 + [pltpu.VMEM((2, 3, 16, 5...  1.88 us
  transfers between devices with their start and end apart: 16, of which 5 were waited for; matrix products, arithmetic and copies ran while one was open for 0% of the time, Pallas kernels for 4%

profile of v1, /device:TPU:2, one launch (start us, length us, event | category | flops | bytes accessed | tf_op | source)
XLA Modules:
  0.0 80.3 jit_solution(9631735176160434984)
XLA Ops:
  0.0 1.9 %first.1 = (bf16[16,16,128]{2,1,0:T(8,128)(2,1)S(1)}, bf16[16,16,128]{2,1,0:T(8,128)(2,1)S(1)}, bf16[2,3,16,576]{3,2,1,0:T(8,128)(2,1)S(1)}, bf16[2,3,16,576]{3,...) custom-call(bf16[16,2,16,128]{3,2,1,0:T(8,128)(2,1)} %density_hbm.1,, ...), custom_call_target="tpu_custom_call" | custom-call | tf_op jit(solution)/shard_map/first/pallas_call | solution.py:202
  1.9 2.7 %collective-permute-start.3 = (bf16[16,16,128]{2,1,0:T(8,128)(2,1)S(1)}, bf16[16,16,128]{2,1,0:T(8,128)(2,1)S(1)}, u32[]{:S(2)}, u32[]{:S(2)}) collective-permute-start(bf16[16,16,128]{2,1,0:T(8,128)(2,1)S(1)} %get-tuple-element.38.outer_ref), channel_id=1, source_target_pairs={{0,240},{16,32},{32,16},{48,64},{64,48},{80,96},{96,80},{112,128},... | collective-permute-start | bytes 196616 | tf_op jit(solution)/shard_map/ppermute | solution.py:169
  4.6 1.9 %collective-permute-start = (bf16[2,3,16,576]{3,2,1,0:T(8,128)(2,1)S(1)}, bf16[2,3,16,576]{3,2,1,0:T(8,128)(2,1)S(1)}, u32[]{:S(2)}, u32[]{:S(2)}) collective-permute-start(bf16[2,3,16,576]{3,2,1,0:T(8,128)(2,1)S(1)} %get-tuple-element.35), channel_id=1, source_target_pairs={{0,1},{1,0},{2,3},{3,2},{4,5},{5,4},{6,7},{7,6},{8,9},{9,8},{10,11... | collective-permute-start | bytes 331784 | tf_op jit(solution)/shard_map/ppermute | solution.py:159
  6.5 0.7 collective-permute-start.1
  7.2 0.9 %collective-permute-start.2 = (bf16[2,3,16,576]{3,2,1,0:T(8,128)(2,1)S(1)}, bf16[2,3,16,576]{3,2,1,0:T(8,128)(2,1)S(1)}, u32[]{:S(2)}, u32[]{:S(2)}) collective-permute-start(bf16[2,3,16,576]{3,2,1,0:T(8,128)(2,1)S(1)} %get-tuple-element.37), channel_id=1, source_target_pairs={{0,9},{1,8},{2,11},{3,10},{4,13},{5,12},{6,15},{7,14},{8,1},{9,0},... | collective-permute-start | bytes 331784 | tf_op jit(solution)/shard_map/ppermute | solution.py:159
  8.1 0.0 collective-permute-done.3.beyond_ref
  8.1 24.8 %all-gather = bf16[12,16,16,128]{3,2,1,0:T(8,128)(2,1)S(1)} all-gather(bf16[3,16,16,128]{3,2,1,0:T(8,128)(2,1)S(1)} %join.1), channel_id=2, replica_groups={{0,2,4,6},{1,3,5,7},{8,10,12,14},{9,11,13,15},{16,18,20,22},{17,19,21,2..., dimensions={0}, use_global_device_ids=true | all-gather | bytes 983040 | tf_op jit(solution)/shard_map/all_gather | solution.py:165
  32.9 0.0 collective-permute-done.w1
  32.9 0.0 collective-permute-done.1.w2
  32.9 0.0 collective-permute-done.2.w3
  33.0 0.1 collective-permute-start.4
  33.1 0.9 %outside.2 = (f32[1,16,16,128]{3,2,1,0:T(8,128)S(1)}, bf16[1,16,16,128]{3,2,1,0:T(8,128)(2,1)S(1)}, bf16[1,16,16,128]{3,2,1,0:T(8,128)(2,1)S(1)}, bf16[1,16,16,1...) custom-call(bf16[4,3,16,16,128]{4,3,2,1,0:T(8,128)(2,1)S(1)} %bitcast.13, bf16[2,3,16,576]{3,2,1,0:T(8,128)(2,1)S(1)} %get-tuple-element.41.w0, ...), custom_call_target="tpu_custom_call" | custom-call | tf_op jit(solution)/shard_map/outside/pallas_call | solution.py:178
  34.0 0.1 collective-permute-start.10
  34.1 1.5 %collective-permute-start.8 = (bf16[1,16,16,128]{3,2,1,0:T(8,128)(2,1)S(1)}, bf16[1,16,16,128]{3,2,1,0:T(8,128)(2,1)S(1)}, u32[]{:S(2)}, u32[]{:S(2)}) collective-permute-start(bf16[1,16,16,128]{3,2,1,0:T(8,128)(2,1)S(1)} %get-tuple-element.52), channel_id=1, source_target_pairs={{0,1},{1,0},{2,3},{3,2},{4,5},{5,4},{6,7},{7,6},{8,9},{9,8},{10,11... | collective-permute-start | bytes 196616 | tf_op jit(solution)/shard_map/ppermute | solution.py:159
  35.6 2.0 %collective-permute-start.9 = (bf16[1,16,16,128]{3,2,1,0:T(8,128)(2,1)S(1)}, bf16[1,16,16,128]{3,2,1,0:T(8,128)(2,1)S(1)}, u32[]{:S(2)}, u32[]{:S(2)}) collective-permute-start(bf16[1,16,16,128]{3,2,1,0:T(8,128)(2,1)S(1)} %get-tuple-element.53), channel_id=1, source_target_pairs={{0,8},{1,9},{2,10},{3,11},{4,12},{5,13},{6,14},{7,15},{8,0},{9,1},... | collective-permute-start | bytes 196616 | tf_op jit(solution)/shard_map/ppermute | solution.py:159
  37.6 0.0 collective-permute-done.4.beside_ref
  37.6 0.9 %inside.2 = (f32[1,16,16,128]{3,2,1,0:T(8,128)S(1)}, f32[1,16,16,128]{3,2,1,0:T(8,128)S(1)}, f32[1,16,16,128]{3,2,1,0:T(8,128)S(1)}, f32[1,16,16,128]{3,2,1,0:T(8,128)S(1)}) custom-call(bf16[576,2048]{1,0:T(8,128)(2,1)S(1)} %get-tuple-element.45.share, bf16[4,16,16,128]{3,2,1,0:T(8,128)(2,1)S(1)} %collective-permute-done.4.beside_ref, ...), custom_call_target="tpu_custom_call" | custom-call | tf_op jit(solution)/shard_map/inside/pallas_call | solution.py:189
  38.5 0.1 collective-permute-start.5
  38.6 0.7 collective-permute-start.6
  39.2 0.6 collective-permute-done.10.p3
  39.9 2.2 %collective-permute-start.7 = (f32[1,16,16,128]{3,2,1,0:T(8,128)S(1)}, f32[1,16,16,128]{3,2,1,0:T(8,128)S(1)}, u32[]{:S(2)}, u32[]{:S(2)}) collective-permute-start(f32[1,16,16,128]{3,2,1,0:T(8,128)S(1)} %get-tuple-element.49), channel_id=1, source_target_pairs={{0,9},{1,8},{2,11},{3,10},{4,13},{5,12},{6,15},{7,14},{8,1},{9,0},... | collective-permute-start | bytes 393224 | tf_op jit(solution)/shard_map/ppermute | solution.py:159
  42.1 0.0 collective-permute-done.8.p1
  42.1 0.0 collective-permute-done.9.p2
  42.1 0.1 outer.1.outer_ref
  42.1 0.1 collective-permute-start.11
  42.2 6.2 %collective-permute-done.11.beyond_ref = bf16[16,16,128]{2,1,0:T(8,128)(2,1)S(1)} collective-permute-done((bf16[16,16,128]{2,1,0:T(8,128)(2,1)S(1)}, bf16[16,16,128]{2,1,0:T(8,128)(2,1)S(1)}, u32[]{:S(2)}, u32[]{:S(2)}) %collective-permute-start.11) | collective-permute-done | bytes 65568 | tf_op jit(solution)/shard_map/ppermute | solution.py:169
  48.4 0.0 collective-permute-done.5.p1
  48.4 0.0 collective-permute-done.6.p2
  48.4 0.0 collective-permute-done.7.p3
  48.4 0.1 inner.1
  48.5 20.1 %all-gather.1 = bf16[12,16,16,128]{3,2,1,0:T(8,128)(2,1)S(1)} all-gather(bf16[3,16,16,128]{3,2,1,0:T(8,128)(2,1)S(1)} %inner.1), channel_id=3, replica_groups={{0,2,4,6},{1,3,5,7},{8,10,12,14},{9,11,13,15},{16,18,20,22},{17,19,21,2..., dimensions={0}, use_global_device_ids=true | all-gather | bytes 983040 | tf_op jit(solution)/shard_map/all_gather | solution.py:165
  68.6 0.1 collective-permute-start.12
  68.7 1.3 %outside.3 = (f32[2,16,16,128]{3,2,1,0:T(8,128)S(1)}, bf16[2,16,16,128]{3,2,1,0:T(8,128)(2,1)S(1)}, bf16[2,16,16,128]{3,2,1,0:T(8,128)(2,1)S(1)}, bf16[2,16,16,128]{3,2,1,0:T(8,128)(2,1)S(1)}, f32[192,2048]{1,0:T(8,128)S(1)}) custom-call(bf16[4,3,16,16,128]{4,3,2,1,0:T(8,128)(2,1)S(1)} %bitcast.15, bf16[2,3,16,576]{3,2,1,0:T(8,128)(2,1)S(1)} %get-tuple-element.41.w0, ...), custom_call_target="tpu_custom_call" | custom-call | tf_op jit(solution)/shard_map/outside/pallas_call | solution.py:178
  70.1 0.2 collective-permute-done.12.beside_ref
  70.3 0.5 inside.3
  70.7 0.1 collective-permute-start.13
  70.9 0.3 collective-permute-start.14
  71.1 3.2 %collective-permute-start.15 = (bf16[2,16,16,128]{3,2,1,0:T(8,128)(2,1)S(1)}, bf16[2,16,16,128]{3,2,1,0:T(8,128)(2,1)S(1)}, u32[]{:S(2)}, u32[]{:S(2)}) collective-permute-start(bf16[2,16,16,128]{3,2,1,0:T(8,128)(2,1)S(1)} %get-tuple-element.63), channel_id=1, source_target_pairs={{0,9},{1,8},{2,11},{3,10},{4,13},{5,12},{6,15},{7,14},{8,1},{9,0},... | collective-permute-start | bytes 393224 | tf_op jit(solution)/shard_map/ppermute | solution.py:159
  74.3 2.8 %collective-permute-done.13.p1 = bf16[2,16,16,128]{3,2,1,0:T(8,128)(2,1)S(1)} collective-permute-done((bf16[2,16,16,128]{3,2,1,0:T(8,128)(2,1)S(1)}, bf16[2,16,16,128]{3,2,1,0:T(8,128)(2,1)S(1)}, u32[]{:S(2)}, u32[]{:S(2)}) %collective-permute-start.13) | collective-permute-done | bytes 131104 | tf_op jit(solution)/shard_map/ppermute | solution.py:159
  77.2 2.3 %collective-permute-done.14.p2 = bf16[2,16,16,128]{3,2,1,0:T(8,128)(2,1)S(1)} collective-permute-done((bf16[2,16,16,128]{3,2,1,0:T(8,128)(2,1)S(1)}, bf16[2,16,16,128]{3,2,1,0:T(8,128)(2,1)S(1)}, u32[]{:S(2)}, u32[]{:S(2)}) %collective-permute-start.14) | collective-permute-done | bytes 131104 | tf_op jit(solution)/shard_map/ppermute | solution.py:159
  79.5 0.0 collective-permute-done.15.p3
  79.5 0.8 %features.1 = f32[16,2,16,128]{3,2,1,0:T(8,128)} custom-call(f32[2,16,16,128]{3,2,1,0:T(8,128)S(1)} %get-tuple-element.60.p0, bf16[2,16,16,128]{3,2,1,0:T(8,128)(2,1)S(1)} %collective-permute-done.13.p1, bf16[2,16,16,128]{3,2,1,0:T(8,128)(2,1)S(1)} %collective-permute-done.14.p2, bf16[2,16,16,128]{3,2,1,0:T(8,128)(2,1)S(1)} %collective-permute-done.15.p3, ...), custom_call_target="tpu_custom_call" | custom-call | tf_op jit(solution)/shard_map/features/pallas_call | solution.py:238
  (3 shorter events, 0.1 us)
Async XLA Ops:
  1.9 6.2 %collective-permute-start.3 = (bf16[16,16,128]{2,1,0:T(8,128)(2,1)S(1)}, bf16[16,16,128]{2,1,0:T(8,128)(2,1)S(1)}, u32[]{:S(2)}, u32[]{:S(2)}) collective-permute-start(bf16[16,16,128]{2,1,0:T(8,128)(2,1)S(1)} %get-tuple-element.38.outer_ref), channel_id=1, source_target_pairs={{0,240},{16,32},{32,16},{48,64},{64,48},{80,96},{96,80},{112,128},... | collective-permute-start | bytes 196616 | tf_op jit(solution)/shard_map/ppermute | solution.py:169
  4.6 28.4 %collective-permute-start = (bf16[2,3,16,576]{3,2,1,0:T(8,128)(2,1)S(1)}, bf16[2,3,16,576]{3,2,1,0:T(8,128)(2,1)S(1)}, u32[]{:S(2)}, u32[]{:S(2)}) collective-permute-start(bf16[2,3,16,576]{3,2,1,0:T(8,128)(2,1)S(1)} %get-tuple-element.35), channel_id=1, source_target_pairs={{0,1},{1,0},{2,3},{3,2},{4,5},{5,4},{6,7},{7,6},{8,9},{9,8},{10,11... | collective-permute-start | bytes 331784 | tf_op jit(solution)/shard_map/ppermute | solution.py:159
  6.5 26.4 %collective-permute-start.1 = (bf16[2,3,16,576]{3,2,1,0:T(8,128)(2,1)S(1)}, bf16[2,3,16,576]{3,2,1,0:T(8,128)(2,1)S(1)}, u32[]{:S(2)}, u32[]{:S(2)}) collective-permute-start(bf16[2,3,16,576]{3,2,1,0:T(8,128)(2,1)S(1)} %get-tuple-element.36), channel_id=1, source_target_pairs={{0,8},{1,9},{2,10},{3,11},{4,12},{5,13},{6,14},{7,15},{8,0},{9,1},... | collective-permute-start | bytes 331784 | tf_op jit(solution)/shard_map/ppermute | solution.py:159
  7.2 25.8 %collective-permute-start.2 = (bf16[2,3,16,576]{3,2,1,0:T(8,128)(2,1)S(1)}, bf16[2,3,16,576]{3,2,1,0:T(8,128)(2,1)S(1)}, u32[]{:S(2)}, u32[]{:S(2)}) collective-permute-start(bf16[2,3,16,576]{3,2,1,0:T(8,128)(2,1)S(1)} %get-tuple-element.37), channel_id=1, source_target_pairs={{0,9},{1,8},{2,11},{3,10},{4,13},{5,12},{6,15},{7,14},{8,1},{9,0},... | collective-permute-start | bytes 331784 | tf_op jit(solution)/shard_map/ppermute | solution.py:159
  33.0 4.6 %collective-permute-start.4 = (bf16[4,16,16,128]{3,2,1,0:T(8,128)(2,1)S(1)}, bf16[4,16,16,128]{3,2,1,0:T(8,128)(2,1)S(1)}, u32[]{:S(2)}, u32[]{:S(2)}) collective-permute-start(bf16[4,16,16,128]{3,2,1,0:T(8,128)(2,1)S(1)} %slice_bitcast_fusion.1), channel_id=1, source_target_pairs={{0,16},{16,0},{32,48},{48,32},{64,80},{80,64},{96,112},{112,96},{1... | collective-permute-start | bytes 786440 | tf_op jit(solution)/shard_map/ppermute | solution.py:227
  34.0 5.9 %collective-permute-start.10 = (bf16[1,16,16,128]{3,2,1,0:T(8,128)(2,1)S(1)}, bf16[1,16,16,128]{3,2,1,0:T(8,128)(2,1)S(1)}, u32[]{:S(2)}, u32[]{:S(2)}) collective-permute-start(bf16[1,16,16,128]{3,2,1,0:T(8,128)(2,1)S(1)} %get-tuple-element.54), channel_id=1, source_target_pairs={{0,9},{1,8},{2,11},{3,10},{4,13},{5,12},{6,15},{7,14},{8,1},{9,0},... | collective-permute-start | bytes 196616 | tf_op jit(solution)/shard_map/ppermute | solution.py:159
  34.1 8.0 %collective-permute-start.8 = (bf16[1,16,16,128]{3,2,1,0:T(8,128)(2,1)S(1)}, bf16[1,16,16,128]{3,2,1,0:T(8,128)(2,1)S(1)}, u32[]{:S(2)}, u32[]{:S(2)}) collective-permute-start(bf16[1,16,16,128]{3,2,1,0:T(8,128)(2,1)S(1)} %get-tuple-element.52), channel_id=1, source_target_pairs={{0,1},{1,0},{2,3},{3,2},{4,5},{5,4},{6,7},{7,6},{8,9},{9,8},{10,11... | collective-permute-start | bytes 196616 | tf_op jit(solution)/shard_map/ppermute | solution.py:159
  35.6 6.5 %collective-permute-start.9 = (bf16[1,16,16,128]{3,2,1,0:T(8,128)(2,1)S(1)}, bf16[1,16,16,128]{3,2,1,0:T(8,128)(2,1)S(1)}, u32[]{:S(2)}, u32[]{:S(2)}) collective-permute-start(bf16[1,16,16,128]{3,2,1,0:T(8,128)(2,1)S(1)} %get-tuple-element.53), channel_id=1, source_target_pairs={{0,8},{1,9},{2,10},{3,11},{4,12},{5,13},{6,14},{7,15},{8,0},{9,1},... | collective-permute-start | bytes 196616 | tf_op jit(solution)/shard_map/ppermute | solution.py:159
  38.5 9.9 %collective-permute-start.5 = (f32[1,16,16,128]{3,2,1,0:T(8,128)S(1)}, f32[1,16,16,128]{3,2,1,0:T(8,128)S(1)}, u32[]{:S(2)}, u32[]{:S(2)}) collective-permute-start(f32[1,16,16,128]{3,2,1,0:T(8,128)S(1)} %get-tuple-element.47), channel_id=1, source_target_pairs={{0,1},{1,0},{2,3},{3,2},{4,5},{5,4},{6,7},{7,6},{8,9},{9,8},{10,11... | collective-permute-start | bytes 393224 | tf_op jit(solution)/shard_map/ppermute | solution.py:159
  38.6 9.8 %collective-permute-start.6 = (f32[1,16,16,128]{3,2,1,0:T(8,128)S(1)}, f32[1,16,16,128]{3,2,1,0:T(8,128)S(1)}, u32[]{:S(2)}, u32[]{:S(2)}) collective-permute-start(f32[1,16,16,128]{3,2,1,0:T(8,128)S(1)} %get-tuple-element.48), channel_id=1, source_target_pairs={{0,8},{1,9},{2,10},{3,11},{4,12},{5,13},{6,14},{7,15},{8,0},{9,1},... | collective-permute-start | bytes 393224 | tf_op jit(solution)/shard_map/ppermute | solution.py:159
  39.9 8.5 %collective-permute-start.7 = (f32[1,16,16,128]{3,2,1,0:T(8,128)S(1)}, f32[1,16,16,128]{3,2,1,0:T(8,128)S(1)}, u32[]{:S(2)}, u32[]{:S(2)}) collective-permute-start(f32[1,16,16,128]{3,2,1,0:T(8,128)S(1)} %get-tuple-element.49), channel_id=1, source_target_pairs={{0,9},{1,8},{2,11},{3,10},{4,13},{5,12},{6,15},{7,14},{8,1},{9,0},... | collective-permute-start | bytes 393224 | tf_op jit(solution)/shard_map/ppermute | solution.py:159
  42.1 6.3 %collective-permute-start.11 = (bf16[16,16,128]{2,1,0:T(8,128)(2,1)S(1)}, bf16[16,16,128]{2,1,0:T(8,128)(2,1)S(1)}, u32[]{:S(2)}, u32[]{:S(2)}) collective-permute-start(bf16[16,16,128]{2,1,0:T(8,128)(2,1)S(1)} %outer.1.outer_ref), channel_id=1, source_target_pairs={{0,240},{16,32},{32,16},{48,64},{64,48},{80,96},{96,80},{112,128},... | collective-permute-start | bytes 196616 | tf_op jit(solution)/shard_map/ppermute | solution.py:169
  68.6 1.6 %collective-permute-start.12 = (bf16[4,16,16,128]{3,2,1,0:T(8,128)(2,1)S(1)}, bf16[4,16,16,128]{3,2,1,0:T(8,128)(2,1)S(1)}, u32[]{:S(2)}, u32[]{:S(2)}) collective-permute-start(bf16[4,16,16,128]{3,2,1,0:T(8,128)(2,1)S(1)} %slice_bitcast_fusion), channel_id=1, source_target_pairs={{0,16},{16,0},{32,48},{48,32},{64,80},{80,64},{96,112},{112,96},{1... | collective-permute-start | bytes 786440 | tf_op jit(solution)/shard_map/ppermute | solution.py:234
  70.7 6.4 %collective-permute-start.13 = (bf16[2,16,16,128]{3,2,1,0:T(8,128)(2,1)S(1)}, bf16[2,16,16,128]{3,2,1,0:T(8,128)(2,1)S(1)}, u32[]{:S(2)}, u32[]{:S(2)}) collective-permute-start(bf16[2,16,16,128]{3,2,1,0:T(8,128)(2,1)S(1)} %get-tuple-element.61), channel_id=1, source_target_pairs={{0,1},{1,0},{2,3},{3,2},{4,5},{5,4},{6,7},{7,6},{8,9},{9,8},{10,11... | collective-permute-start | bytes 393224 | tf_op jit(solution)/shard_map/ppermute | solution.py:159
  70.9 8.6 %collective-permute-start.14 = (bf16[2,16,16,128]{3,2,1,0:T(8,128)(2,1)S(1)}, bf16[2,16,16,128]{3,2,1,0:T(8,128)(2,1)S(1)}, u32[]{:S(2)}, u32[]{:S(2)}) collective-permute-start(bf16[2,16,16,128]{3,2,1,0:T(8,128)(2,1)S(1)} %get-tuple-element.62), channel_id=1, source_target_pairs={{0,8},{1,9},{2,10},{3,11},{4,12},{5,13},{6,14},{7,15},{8,0},{9,1},... | collective-permute-start | bytes 393224 | tf_op jit(solution)/shard_map/ppermute | solution.py:159
  71.1 8.4 %collective-permute-start.15 = (bf16[2,16,16,128]{3,2,1,0:T(8,128)(2,1)S(1)}, bf16[2,16,16,128]{3,2,1,0:T(8,128)(2,1)S(1)}, u32[]{:S(2)}, u32[]{:S(2)}) collective-permute-start(bf16[2,16,16,128]{3,2,1,0:T(8,128)(2,1)S(1)} %get-tuple-element.63), channel_id=1, source_target_pairs={{0,9},{1,8},{2,11},{3,10},{4,13},{5,12},{6,15},{7,14},{8,1},{9,0},... | collective-permute-start | bytes 393224 | tf_op jit(solution)/shard_map/ppermute | solution.py:159
